TPU v7x, 32 devices: a whole 2x2x4 slice. The times are simulated.
32 devices in a mesh: row: 4 (over y, core), col: 8 (over z, x).
Axes of the slice: x: 2, y: 2, z: 4, core: 2. Of those that a mesh axis runs over, the one named last changes fastest.
Arguments:
- theta: float32 [32, 256, 256], P('row', None, 'col'), may hold values from -6 to 6
- left_env: float32 [16, 32, 256, 256], P('row', 'col'), as said below
- right_env: float32 [8, 32, 256, 256], P(None, 'col'), as said below
- left_sector: int32 [32], replicated, may hold values from 0 to 15, as said below
- right_sector: int32 [32], P('row'), may hold values from 0 to 7
- term_on: int32 [32, 32], P('row', 'col'), may hold values 0 or 1
- left_size: int32 [16], replicated, may hold values from 1 to 256, 2560 in all
- right_size: int32 [8], replicated, may hold values from 1 to 256, 1280 in all
Outputs:
- new_theta: float32 [32, 256, 256], P('row', None, 'col')
- energy: float32 [], replicated
Inputs may be any that keep to these rules, and one draw needn't show every extreme that they name: `left_sector`: left sector s belongs to row s // 4. Block k belongs to row k // 8. The 8 blocks of one row name distinct left sectors; they name either none or exactly 4 sectors belonging to any one row, and the blocks of every row name 4 sectors belonging to one common row. `left_env`: each tile is symmetric in its last two dimensions. `right_env`: each tile is symmetric in its last two dimensions.
All inputs are finite; a program needn't handle non-finite values. No bound on the sum of `term_on` on one device may be relied on, other than what follows from the above.
Results may differ from a plain program's by a relative error of at most 0.0001.
Values sent between devices are 32-bit elements; how exact they have to be, the bound alone decides.
A program may use at most 128 MiB of HBM per device.

v0:
```python
import jax
import jax.numpy as jnp
from jax import lax
from jax.sharding import PartitionSpec as P

ITERS = 2


highest = lax.Precision.HIGHEST


def lookup(small_table, index_list):
    slot_hits = index_list[:, None] == jnp.arange(small_table.shape[0], dtype=jnp.int32)[None, :]
    return jnp.sum(jnp.where(slot_hits, small_table[None, :], 0), axis=1)


def tile_masks(left_ids, right_ids, left_size, right_size, tile_size, offset, span_cols):
    rows_live = lookup(left_size, left_ids)
    cols_live = lookup(right_size, right_ids)
    row_mask = (jnp.arange(tile_size, dtype=jnp.int32)[None, :] < rows_live[:, None]).astype(
        jnp.float32
    )
    col_mask = (
        (offset + jnp.arange(span_cols, dtype=jnp.int32))[None, :] < cols_live[:, None]
    ).astype(jnp.float32)
    return row_mask[:, :, None] * col_mask[:, None, :]


def local(theta, left_env, right_env, left_sector, right_sector, term_on, left_size, right_size):
    row_count = lax.axis_size("row")
    blocks, tile_size, thin_cols = theta.shape
    local_sectors = left_env.shape[0]
    capacity = max(2, 2 * blocks // row_count)
    row_index = lax.axis_index("row")
    col_index = lax.axis_index("col")
    own_left = lax.dynamic_slice_in_dim(left_sector, row_index * blocks, blocks)
    offset = col_index * thin_cols
    span_cols = theta.shape[2]
    start_mask = tile_masks(
        own_left, right_sector, left_size, right_size, tile_size, offset, span_cols
    )
    start_vec = theta * start_mask
    senders = row_index * local_sectors + jnp.arange(local_sectors, dtype=jnp.int32)
    wanted = left_sector.reshape(row_count, blocks)
    used_flag = jnp.any(wanted[:, :, None] == senders[None, None, :], axis=1)
    used_count = used_flag.astype(jnp.int32)
    before = jnp.cumsum(used_count, axis=1) - used_count
    pick_flag = used_flag[:, None, :] & (
        before[:, None, :] == jnp.arange(capacity, dtype=jnp.int32)[None, :, None]
    )
    filled = jnp.any(pick_flag, axis=2).reshape(-1)
    local_index = jnp.sum(
        jnp.where(pick_flag, jnp.arange(local_sectors, dtype=jnp.int32)[None, None, :], 0), axis=2
    ).reshape(-1)
    outgoing = (
        jnp.take(left_env, local_index, axis=0) * filled.astype(jnp.float32)[:, None, None, None]
    )
    arrived = lax.all_to_all(outgoing, "row", split_axis=0, concat_axis=0, tiled=True)
    every_sector = jnp.arange(row_count * local_sectors, dtype=jnp.int32)
    needed = (
        jnp.any(own_left[:, None] == every_sector[None, :], axis=0)
        .astype(jnp.int32)
        .reshape(row_count, local_sectors)
    )
    order_rank = (jnp.cumsum(needed, axis=1) - needed).reshape(-1)
    position = own_left // local_sectors * capacity + lookup(order_rank, own_left)
    left_pick = jnp.take(arrived, position, axis=0)
    right_pick = jnp.take(right_env, right_sector, axis=0)
    weights = term_on.astype(jnp.float32)

    def contract(full_vector):
        middle = (
            jnp.einsum("swia,sab->swib", left_pick, full_vector, precision=highest)
            * weights[:, :, None, None]
        )
        return jnp.einsum("swib,swjb->sij", middle, right_pick, precision=highest)

    def operate(vector):
        full_vector = lax.all_gather(vector, "col", axis=2, tiled=True)
        total_sum = lax.psum_scatter(contract(full_vector), "col", scatter_dimension=2, tiled=True)
        return total_sum * start_mask

    def combine(values):
        reduced = lax.psum(values, ("row", "col"))
        return reduced

    image_vec = operate(start_vec)
    norm_sq, correlation = combine((jnp.sum(start_vec * start_vec), jnp.sum(start_vec * image_vec)))
    inv_norm = 1.0 / jnp.sqrt(norm_sq)
    basis_vec = start_vec * inv_norm
    applied = image_vec * inv_norm
    ritz_value = correlation / norm_sq
    for turn_index in range(ITERS):
        residual = applied - ritz_value * basis_vec
        (res_sq,) = combine((jnp.sum(residual * residual),))
        length = jnp.sqrt(res_sq)
        fresh_vec = residual / length
        fresh_applied = operate(fresh_vec)
        (curvature,) = combine((jnp.sum(fresh_vec * fresh_applied),))
        half_gap = 0.5 * (ritz_value - curvature)
        root_term = jnp.sqrt(half_gap * half_gap + res_sq)
        lowest = 0.5 * (ritz_value + curvature) - root_term
        first_coef = curvature - lowest
        pair_norm = jnp.sqrt(first_coef * first_coef + res_sq)
        basis_vec = (first_coef * basis_vec - length * fresh_vec) / pair_norm
        applied = (first_coef * applied - length * fresh_applied) / pair_norm
        ritz_value = lowest
    total_entries = blocks * row_count * tile_size * tile_size
    output = basis_vec * jnp.sqrt(jnp.float32(total_entries))
    return (output, ritz_value)


def solution(mesh):
    placed = (
        P("row", None, "col"),
        P("row", "col", None, None),
        P(None, "col", None, None),
        P(),
        P("row"),
        P("row", "col"),
        P(),
        P(),
    )
    return jax.shard_map(
        local, mesh=mesh, in_specs=placed, out_specs=(P("row", None, "col"), P()), check_vma=False
    )
```

profile of v0, /device:TPU:0, one launch (start us, length us, event | category | flops | bytes accessed | tf_op | source)
XLA Modules:
  0.0 833.7 jit_solution(15604746448957152771)
XLA Ops:
  9.0 9.9 %gather_fusion = f32[16,4,256,256]{3,2,1,0:T(8,128)} fusion(f32[4,4,256,256]{3,2,1,0:T(8,128)} %param.9, s32[1024]{0:T(1024)S(1)} %pad_clamp_fusion.2), kind=kCustom, calls=%fused_computation | custom fusion | bytes 33554496 | tf_op jit(solution)/shard_map/jit(_take)/gather | solution.py:56
  18.9 11.6 %select_multiply_fusion = f32[16,4,256,256]{3,2,1,0:T(8,128)} fusion(f32[16,4,256,256]{3,2,1,0:T(8,128)} %gather_fusion, f32[16]{0:T(128)S(1)} %reshape.149, pred[16]{0:T(512)(128)(4,1)S(1)} %compare_and_fusion.1), kind=kLoop, calls=%fused_computation.3 | loop fusion | flops 8388608 | bytes 33554512 | tf_op jit(solution)/shard_map/mul | solution.py:56
  30.5 7.1 all-to-all-start
  39.9 7.7 gather_fusion.2
  47.7 173.6 %all-to-all-done = f32[16,4,256,256]{3,2,1,0:T(8,128)} async-done(((f32[16,4,256,256]{3,2,1,0:T(8,128)}), f32[16,4,256,256]{3,2,1,0:T(8,128)}, u32[]{:S(2)}, u32[]{:S(2)}) %all-to-all-start) | async-done | bytes 16777248 | tf_op jit(solution)/shard_map/all_to_all | solution.py:58
  221.3 10.1 %gather_fusion.1 = f32[8,4,256,256]{3,2,1,0:T(8,128)} fusion(f32[16,4,256,256]{3,2,1,0:T(8,128)} %all-to-all-done, s32[1024]{0:T(1024)S(1)} %pad_clamp_fusion.1), kind=kCustom, calls=%fused_computation.1 | custom fusion | bytes 16777248 | tf_op jit(solution)/shard_map/jit(_take)/gather | solution.py:67
  231.4 13.2 %fusion.13 = f32[8,4,256,256]{3,2,1,0:T(8,128)} fusion(f32[8,4,256,256]{3,2,1,0:T(8,128)} %gather_fusion.1, pred[8]{0:T(512)(128)(4,1)S(1)} %get-tuple-element.10, f32[8,256,256]{1,2,0:T(8,128)} %all-gather.4.cloned.1.call-done), kind=kOutput, calls=%fused_computation.17 | convolution fusion | flops 6444548096 | bytes 18874376 | tf_op jit(solution)/shard_map/swia,sab->swib/dot_general | solution.py:73
  244.6 12.3 %fusion.33 = f32[8,256,256]{1,2,0:T(8,128)} fusion(f32[8,4,256,256]{3,2,1,0:T(8,128)S(1)} %copy-done, pred[8]{0:T(512)(128)(4,1)S(1)} %compare_and_fusion, f32[8,4,256,256]{3,2,1,0:T(8,128)} %fusion.13, f32[8,4]{1,0:T(8,128)S(1)} %copy.11), kind=kOutput, calls=%fused_computation.37 | convolution fusion | flops 6446645248 | bytes 18874504 | tf_op jit(solution)/shard_map/swib,swjb->sij/dot_general | solution.py:76
  257.0 68.8 %reduce-scatter.4.cloned.1.call-done = f32[8,256,32]{1,2,0:T(8,128)} async-done(((f32[8,256,256]{1,2,0:T(8,128)}), f32[8,256,32]{1,2,0:T(8,128)}) %reduce-scatter.4.cloned.1.call-update) | async-done | bytes 262160 | tf_op jit(solution)/shard_map/reduce_scatter | solution.py:80
  327.5 39.8 %all-reduce = (f32[]{:T(128)}, f32[]{:T(128)}) all-reduce(f32[]{:T(128)} %get-tuple-element.3, f32[]{:T(128)} %get-tuple-element.2), channel_id=1, replica_groups=mesh['row'=4,'col'=8] {'row','col'}, use_global_device_ids=true, to_apply=%region_13.14 | all-reduce | flops 2 | bytes 16 | tf_op jit(solution)/shard_map/psum | solution.py:84
  371.0 40.2 %psum.44 = f32[]{:T(128)} all-reduce(f32[]{:T(128)} %multiply_reduce_fusion.2), channel_id=1, replica_groups=mesh['row'=4,'col'=8] {'row','col'}, use_global_device_ids=true, to_apply=%region_15.16 | all-reduce | flops 1 | bytes 8 | tf_op jit(solution)/shard_map/psum | solution.py:84
  411.8 1.8 broadcast_divide_fusion.1
  413.7 49.5 %all-gather.6.cloned.1.call-done = f32[8,256,256]{1,2,0:T(8,128)} async-done(((f32[8,256,32]{1,2,0:T(8,128)}), f32[8,256,256]{1,2,0:T(8,128)}) %all-gather.6.cloned.1.call-update) | async-done | bytes 2097168 | tf_op jit(solution)/shard_map/all_gather | solution.py:79
  463.2 11.1 %fusion.11 = f32[8,4,256,256]{3,2,1,0:T(8,128)S(1)} fusion(f32[8,4,256,256]{3,2,1,0:T(8,128)} %gather_fusion.1, pred[8]{0:T(512)(128)(4,1)S(1)} %get-tuple-element.10, f32[8,256,256]{1,2,0:T(8,128)} %all-gather.6.cloned.1.call-done), kind=kOutput, calls=%fused_computation.15 | convolution fusion | flops 6444548096 | bytes 18874376 | tf_op jit(solution)/shard_map/swia,sab->swib/dot_general | solution.py:73
  474.3 12.3 %fusion.38 = f32[8,256,256]{1,2,0:T(8,128)} fusion(f32[8,4,256,256]{3,2,1,0:T(8,128)} %gather_fusion.2, pred[8]{0:T(512)(128)(4,1)S(1)} %compare_and_fusion, f32[8,4,256,256]{3,2,1,0:T(8,128)S(1)} %fusion.11, f32[8,4]{1,0:T(8,128)S(1)} %copy.11), kind=kOutput, calls=%fused_computation.38 | convolution fusion | flops 6446645248 | bytes 18874504 | tf_op jit(solution)/shard_map/swib,swjb->sij/dot_general | solution.py:76
  486.7 66.6 %reduce-scatter.6.cloned.1.call-done = f32[8,256,32]{1,2,0:T(8,128)} async-done(((f32[8,256,256]{1,2,0:T(8,128)}), f32[8,256,32]{1,2,0:T(8,128)}) %reduce-scatter.6.cloned.1.call-update) | async-done | bytes 262160 | tf_op jit(solution)/shard_map/reduce_scatter | solution.py:80
  554.9 39.8 %psum.45 = f32[]{:T(128)} all-reduce(f32[]{:T(128)} %multiply_reduce_fusion.1), channel_id=1, replica_groups=mesh['row'=4,'col'=8] {'row','col'}, use_global_device_ids=true, to_apply=%region_18.19 | all-reduce | flops 1 | bytes 8 | tf_op jit(solution)/shard_map/psum | solution.py:84
  598.1 1.8 multiply_reduce_fusion
  599.9 39.9 %psum.46 = f32[]{:T(128)} all-reduce(f32[]{:T(128)} %get-tuple-element.8), channel_id=1, replica_groups=mesh['row'=4,'col'=8] {'row','col'}, use_global_device_ids=true, to_apply=%region_20.21 | all-reduce | flops 1 | bytes 8 | tf_op jit(solution)/shard_map/psum | solution.py:84
  641.5 49.2 %all-gather.8.cloned.1.call-done = f32[8,256,256]{1,2,0:T(8,128)} async-done(((f32[8,256,32]{1,2,0:T(8,128)}), f32[8,256,256]{1,2,0:T(8,128)}) %all-gather.8.cloned.1.call-update) | async-done | bytes 2097168 | tf_op jit(solution)/shard_map/all_gather | solution.py:79
  690.6 11.1 %fusion.9 = f32[8,4,256,256]{3,2,1,0:T(8,128)S(1)} fusion(f32[8,4,256,256]{3,2,1,0:T(8,128)} %gather_fusion.1, pred[8]{0:T(512)(128)(4,1)S(1)} %get-tuple-element.10, f32[8,256,256]{1,2,0:T(8,128)} %all-gather.8.cloned.1.call-done), kind=kOutput, calls=%fused_computation.13 | convolution fusion | flops 6444548096 | bytes 18874376 | tf_op jit(solution)/shard_map/swia,sab->swib/dot_general | solution.py:73
  701.8 12.3 %fusion.43 = f32[8,256,256]{1,2,0:T(8,128)} fusion(f32[8,4,256,256]{3,2,1,0:T(8,128)} %gather_fusion.2, pred[8]{0:T(512)(128)(4,1)S(1)} %compare_and_fusion, f32[8,4,256,256]{3,2,1,0:T(8,128)S(1)} %fusion.9, f32[8,4]{1,0:T(8,128)S(1)} %copy.11), kind=kOutput, calls=%fused_computation.39 | convolution fusion | flops 6446645248 | bytes 18874504 | tf_op jit(solution)/shard_map/swib,swjb->sij/dot_general | solution.py:76
  714.1 66.2 %reduce-scatter.8.cloned.1.call-done = f32[8,256,32]{1,2,0:T(8,128)} async-done(((f32[8,256,256]{1,2,0:T(8,128)}), f32[8,256,32]{1,2,0:T(8,128)}) %reduce-scatter.8.cloned.1.call-update) | async-done | bytes 262160 | tf_op jit(solution)/shard_map/reduce_scatter | solution.py:80
  781.9 39.8 %psum.47 = f32[]{:T(128)} all-reduce(f32[]{:T(128)} %fusion.49), channel_id=1, replica_groups=mesh['row'=4,'col'=8] {'row','col'}, use_global_device_ids=true, to_apply=%region_23.24 | all-reduce | flops 1 | bytes 8 | tf_op jit(solution)/shard_map/psum | solution.py:84
  (72 shorter events, 13.0 us)
Async XLA Ops:
  30.5 7.2 copy-start.4
  30.5 7.7 copy-start.7
  30.5 7.7 copy-start.8
  30.5 7.9 copy-start.6
  30.5 8.3 copy-start.1
  30.5 9.3 %copy-start.5 = (s32[8,4]{0,1:T(4,128)S(1)}, s32[8,4]{0,1:T(4,128)}, u32[]{:S(2)}) copy-start(s32[8,4]{0,1:T(4,128)} %param.13) | copy-start | bytes 388
  30.5 190.8 %all-to-all-start = ((f32[16,4,256,256]{3,2,1,0:T(8,128)}), f32[16,4,256,256]{3,2,1,0:T(8,128)}, u32[]{:S(2)}, u32[]{:S(2)}) async-start(f32[16,4,256,256]{3,2,1,0:T(8,128)} %select_multiply_fusion), calls=%async_computation | async-start | bytes 33554432 | tf_op jit(solution)/shard_map/all_to_all | solution.py:58
  37.6 193.8 %all-gather.4.cloned.1.call-start = ((), (), s32[]{:S(2)}) async-start(), calls=%async_computation.4 | async-start | bytes 2359296 | tf_op jit(solution)/shard_map/all_gather | solution.py:79
  39.6 286.2 %reduce-scatter.4.cloned.1.call-start = ((), (), s32[]{:S(2)}) async-start(), calls=%async_computation.5 | async-start | bytes 2359296 | tf_op jit(solution)/shard_map/reduce_scatter | solution.py:80
  231.4 13.2 %copy-start = (f32[8,4,256,256]{3,2,1,0:T(8,128)S(1)}, f32[8,4,256,256]{3,2,1,0:T(8,128)}, u32[]{:S(2)}) copy-start(f32[8,4,256,256]{3,2,1,0:T(8,128)} %gather_fusion.2) | copy-start | bytes 25165828
  257.0 206.2 %all-gather.6.cloned.1.call-start = ((), (), s32[]{:S(2)}) async-start(), calls=%async_computation.6 | async-start | bytes 2359296 | tf_op jit(solution)/shard_map/all_gather | solution.py:79
  413.7 139.6 %reduce-scatter.6.cloned.1.call-start = ((), (), s32[]{:S(2)}) async-start(), calls=%async_computation.7 | async-start | bytes 2359296 | tf_op jit(solution)/shard_map/reduce_scatter | solution.py:80
  474.3 78.9 %copy-start.2 = (f32[8,256,32]{1,2,0:T(8,128)S(1)}, f32[8,256,32]{1,2,0:T(8,128)}, u32[]{:S(2)}) copy-start(f32[8,256,32]{1,2,0:T(8,128)} %broadcast_divide_fusion.1) | copy-start | bytes 786436
  474.3 123.7 %copy-start.3 = (f32[8,256,32]{1,2,0:T(8,128)S(1)}, f32[8,256,32]{1,2,0:T(8,128)}, u32[]{:S(2)}) copy-start(f32[8,256,32]{1,2,0:T(8,128)} %reduce-scatter.4.cloned.1.call-done) | copy-start | bytes 786436
  486.6 204.0 %all-gather.8.cloned.1.call-start = ((), (), s32[]{:S(2)}) async-start(), calls=%async_computation.8 | async-start | bytes 2359296 | tf_op jit(solution)/shard_map/all_gather | solution.py:79
  641.2 139.0 %reduce-scatter.8.cloned.1.call-start = ((), (), s32[]{:S(2)}) async-start(), calls=%async_computation.9 | async-start | bytes 2359296 | tf_op jit(solution)/shard_map/reduce_scatter | solution.py:80
Sparse Core Ops, SparseCore 0:
  41.2 52.3 all-gather.3
  257.1 68.6 reduce-scatter.3
  413.8 49.3 all-gather.5
  486.7 66.4 reduce-scatter.5
  641.3 49.2 all-gather.7
  714.2 65.9 reduce-scatter.7
where the time goes:
time: 835 us; the launch traced here: 834 us
  waiting for transfers between devices  474 us (57%)
  blocking collectives  200 us (24%)
  matrix products  72.3 us (9%)
  local copies, waits for them, and re-layouts  29 us (3%)
  other arithmetic  26.1 us (3%)
  between operations  25.2 us (3%)
    reduce_scatter x3, waiting for transfers between devices, operate(): lax.psum_scatter(contract(full_vector), 'col', scatter_dimension=2, tiled...  201 us
    psum x5, blocking collectives, combine(): reduced = lax.psum(values, ('row', 'col'))  200 us
    all_to_all x1, waiting for transfers between devices, local(): lax.all_to_all(outgoing, 'row', split_axis=0, concat_axis=0, tiled=True)  174 us
    all_gather x3, waiting for transfers between devices, operate(): full_vector = lax.all_gather(vector, 'col', axis=2, tiled=True)  98.6 us
    dot_general x3, matrix products, contract(): return jnp.einsum('swib,swjb->sij', middle, right_pick, precision=highest)  36.8 us
    dot_general x3, matrix products, contract(): jnp.einsum('swia,sab->swib', left_pick, full_vector, precision=highest)  35.4 us
  transfers between devices with their start and end apart: 7, of which 6 were waited for; matrix products, arithmetic and copies ran while one was open for 2% of the time, Pallas kernels for 0%

commit v1 on v0

v1 whole, which is shorter than its diff:
```python
import functools

import jax
import jax.numpy as jnp
from jax import lax
from jax.experimental import pallas as pl
from jax.experimental.pallas import tpu as pltpu
from jax.sharding import PartitionSpec as P

ITERS = 2
APPLIES = ITERS + 1
ROUNDS = 2 * ITERS + 1
CORES = 2
MESH = pl.DeviceIdType.MESH


def lookup(small_table, index_list):
    slot_hits = index_list[:, None] == jnp.arange(small_table.shape[0], dtype=jnp.int32)[None, :]
    return jnp.sum(jnp.where(slot_hits, small_table[None, :], 0), axis=1)


def pack_symmetric(tiles):
    half = tiles.shape[-1] // 2
    upper = tiles[..., :half, half:]
    first = tiles[..., :half, :half]
    second = tiles[..., half:, half:]
    rows = lax.broadcasted_iota(jnp.int32, (half, half), 0)
    cols = lax.broadcasted_iota(jnp.int32, (half, half), 1)
    both = jnp.where(rows <= cols, first, second)
    diag = jnp.sum(jnp.where(rows == cols, second, 0.0), axis=-2, keepdims=True)
    fill = jnp.zeros(tiles.shape[:-2] + (7, half), tiles.dtype)
    return jnp.concatenate([upper, both, diag, fill], axis=-2)


def split(x):
    high = x.astype(jnp.bfloat16)
    low = (x - high.astype(jnp.float32)).astype(jnp.bfloat16)
    return high, low


def dot3(a_high, a_low, b_high, b_low):
    mul = functools.partial(jnp.dot, preferred_element_type=jnp.float32)
    return mul(a_high, b_high) + (mul(a_high, b_low) + mul(a_low, b_high))


def tile_sum(x):
    cols = x.shape[-1]
    total = jnp.sum(x.reshape(-1, 8, cols), axis=0)
    return sum(total[:, i : i + 128] for i in range(0, cols, 128))


def kernel(
    n_row,
    n_col,
    total_entries,
    left_ref,
    right_ref,
    weight_ref,
    start_ref,
    mask_ref,
    pack_ref,
    env_ref,
    out_ref,
    energy_ref,
    gathered,
    left_high,
    left_low,
    stage,
    right_high,
    right_low,
    full,
    partial,
    from_right,
    from_left,
    basis,
    applied,
    vector,
    row_sums,
    col_sums,
    env_sem,
    own_sem,
    far_sem,
    near_sem,
    pass_sem,
    gather_sem,
    scatter_sem,
    row_sem,
    col_sem,
):
    blocks, thin, size = start_ref.shape
    sectors, terms = pack_ref.shape[:2]
    half = size // 2
    half_blocks = blocks // 2
    steps = n_col // 2
    n_far = n_row // CORES - 1
    me_row = lax.axis_index("row")
    me_col = lax.axis_index("col")

    def col_at(place):
        place = lax.rem(place + 2 * n_col, n_col)
        back = place // (n_col // 2)
        return (1 - back) * (2 * place) + back * (2 * n_col - 1 - 2 * place)

    odd = lax.rem(me_col, 2)
    place = (1 - odd) * (me_col // 2) + odd * (n_col - 1 - me_col // 2)
    right = col_at(place + 1)
    left = col_at(place - 1)

    def remote(src, dst, sems, row, col):
        return pltpu.make_async_remote_copy(
            src_ref=src,
            dst_ref=dst,
            send_sem=sems.at[0],
            recv_sem=sems.at[1],
            device_id=(row, col),
            device_id_type=MESH,
        )

    barrier = pltpu.get_barrier_semaphore()
    for step in range(1, n_row):
        peer = lax.rem(me_row + step, n_row)
        pl.semaphore_signal(barrier, inc=1, device_id=(peer, me_col), device_id_type=MESH)
    for step in range(1, n_col):
        peer = lax.rem(me_col + step, n_col)
        pl.semaphore_signal(barrier, inc=1, device_id=(me_row, peer), device_id_type=MESH)
    pl.semaphore_wait(barrier, n_row + n_col - 2)

    core = lax.rem(me_row, CORES)
    partner = me_row + 1 - 2 * core

    def sector_slot(row, sector):
        return gathered.at[row * sectors + sector]

    far = []
    for step in range(1, n_far + 1):
        target = lax.rem(me_row + CORES * step, n_row)
        for sector in range(sectors):
            copy = remote(
                pack_ref.at[sector],
                sector_slot(me_row, sector),
                far_sem.at[step - 1, sector],
                target,
                me_col,
            )
            copy.start()
            far.append(copy)
    near = remote(
        pack_ref, gathered.at[pl.ds(me_row * sectors, sectors)], near_sem, partner, me_col
    )
    near.start()
    own = pltpu.make_async_copy(
        pack_ref, gathered.at[pl.ds(me_row * sectors, sectors)], own_sem
    )
    own.start()

    def gather_start(turn):
        full[turn, me_col] = vector[...]

    def gather_step(turn, step):
        last = step == steps - 1
        ahead = col_at(place - step)
        behind = col_at(place + step)
        first_part = pl.ds(0, half_blocks if last else blocks)
        second_part = pl.ds(half_blocks, half_blocks) if last else pl.ds(0, blocks)
        clockwise = full.at[turn, ahead, first_part]
        counter = full.at[turn, behind, second_part]
        pair = (
            remote(clockwise, clockwise, gather_sem.at[turn, step, 0], me_row, right),
            remote(counter, counter, gather_sem.at[turn, step, 1], me_row, left),
        )
        for copy in pair:
            copy.start()
        return pair

    def gather(turn, between):
        gather_start(turn)
        sent = []
        for step in range(steps):
            pair = gather_step(turn, step)
            sent.extend(pair)
            if step == 0:
                between()
            for copy in pair:
                copy.wait_recv()
        for copy in sent:
            copy.wait_send()

    def contract(turn):
        def block_step(block, carry):
            v_high, v_low = split(full[turn, :, block].reshape(size, size))
            sector = right_ref[block]
            total = jnp.zeros((size, size), jnp.float32)
            for term in range(terms):
                spot = block * terms + term
                middle = dot3(v_high, v_low, left_high[spot], left_low[spot])
                m_high, m_low = split(middle * weight_ref[block, term])
                total = total + dot3(
                    right_high[sector, term], right_low[sector, term], m_high, m_low
                )
            partial[:, block] = total.reshape(n_col, thin, size)
            return carry

        lax.fori_loop(0, blocks, block_step, 0)

    def scatter(turn):
        sent = []
        for step in range(steps):
            first = step == 0
            part_one = pl.ds(0, half_blocks if first else blocks)
            part_two = pl.ds(half_blocks, half_blocks) if first else pl.ds(0, blocks)
            low = col_at(place - steps + step)
            high = col_at(place + steps - step)
            if step == 1:
                partial[low, pl.ds(0, half_blocks)] += from_right[turn, 0, pl.ds(0, half_blocks)]
                partial[high, pl.ds(half_blocks, half_blocks)] += from_left[
                    turn, 0, pl.ds(half_blocks, half_blocks)
                ]
            elif step > 1:
                partial[low] += from_right[turn, step - 1]
                partial[high] += from_left[turn, step - 1]
            pair = (
                remote(
                    partial.at[low, part_one],
                    from_right.at[turn, step, part_one],
                    scatter_sem.at[turn, step, 0],
                    me_row,
                    left,
                ),
                remote(
                    partial.at[high, part_two],
                    from_left.at[turn, step, part_two],
                    scatter_sem.at[turn, step, 1],
                    me_row,
                    right,
                ),
            )
            for copy in pair:
                copy.start()
            sent.extend(pair)
            for copy in pair:
                copy.wait_recv()
        for copy in sent:
            copy.wait_send()
        result = partial[me_col] + from_right[turn, steps - 1] + from_left[turn, steps - 1]
        return result * mask_ref[...]

    def combine(index, values):
        count = len(values)
        for i, value in enumerate(values):
            row_sums[index, me_row, i] = tile_sum(value)
        copies = []
        for step in range(1, n_row):
            mine = row_sums.at[index, me_row, pl.ds(0, count)]
            peer = lax.rem(me_row + step, n_row)
            copies.append(remote(mine, mine, row_sem.at[index, step - 1], peer, me_col))
        for copy in copies:
            copy.start()
        for copy in copies:
            copy.wait_recv()
        for i in range(count):
            col_sums[index, me_col, i] = sum(row_sums[index, r, i] for r in range(n_row))
        more = []
        for step in range(1, n_col):
            mine = col_sums.at[index, me_col, pl.ds(0, count)]
            peer = lax.rem(me_col + step, n_col)
            more.append(remote(mine, mine, col_sem.at[index, step - 1], me_row, peer))
        for copy in more:
            copy.start()
        for copy in more:
            copy.wait_recv()
        for copy in copies + more:
            copy.wait_send()
        totals = [sum(col_sums[index, c, i] for c in range(n_col)) for i in range(count)]
        return [jnp.sum(total, axis=(0, 1), keepdims=True) for total in totals]

    def load_right():
        count = env_ref.shape[0]
        copies = [
            pltpu.make_async_copy(env_ref.at[i], stage.at[i % 2], env_sem.at[i % 2])
            for i in range(count)
        ]
        copies[0].start()
        for i in range(count):
            if i + 1 < count:
                copies[i + 1].start()
            copies[i].wait()
            for term in range(terms):
                right_high[i, term], right_low[i, term] = split(stage[i % 2, term])

    def load_left():
        forward = []
        for step in range(1, n_far + 1):
            source = lax.rem(me_row - CORES * step + n_row, n_row)
            for sector in range(sectors):
                far[(step - 1) * sectors + sector].wait_recv()
                slot = sector_slot(source, sector)
                copy = remote(slot, slot, pass_sem.at[step - 1, sector], partner, me_col)
                copy.start()
                forward.append(copy)
        own.wait()
        near.wait_recv()
        for copy in forward:
            copy.wait_recv()
        for copy in far + [near] + forward:
            copy.wait_send()

        rows = lax.broadcasted_iota(jnp.int32, (half, half), 0)
        cols = lax.broadcasted_iota(jnp.int32, (half, half), 1)

        def unpack(block, carry):
            sector = left_ref[block]
            for term in range(terms):
                tile = gathered[sector, term]
                spot = block * terms + term
                upper = tile[:half]
                both = tile[half:size]
                flipped = both.T
                first = jnp.where(rows <= cols, both, flipped)
                second = jnp.where(rows > cols, both, flipped)
                second = jnp.where(rows == cols, tile[size : size + 1], second)
                quarters = (
                    (0, 0, first),
                    (0, half, upper),
                    (half, 0, upper.T),
                    (half, half, second),
                )
                for at_row, at_col, quarter in quarters:
                    high, low = split(quarter)
                    left_high[spot, at_row : at_row + half, at_col : at_col + half] = high
                    left_low[spot, at_row : at_row + half, at_col : at_col + half] = low
            return carry

        lax.fori_loop(0, blocks, unpack, 0)

    vector[...] = start_ref[...]
    gather(0, load_right)
    load_left()
    contract(0)
    image = scatter(0)
    start = start_ref[...]
    norm_sq, correlation = combine(0, (start * start, start * image))
    inv_norm = 1.0 / jnp.sqrt(norm_sq)
    basis[...] = start * inv_norm
    applied[...] = image * inv_norm
    ritz = correlation / norm_sq
    for turn in range(1, ITERS + 1):
        vector[...] = applied[...] - ritz * basis[...]
        found = []

        def between():
            found.extend(combine(2 * turn - 1, (vector[...] * vector[...],)))

        gather(turn, between)
        (res_sq,) = found
        length = jnp.sqrt(res_sq)
        contract(turn)
        fresh_applied = scatter(turn) / length
        fresh = vector[...] / length
        (curvature,) = combine(2 * turn, (fresh * fresh_applied,))
        half_gap = 0.5 * (ritz - curvature)
        root_term = jnp.sqrt(half_gap * half_gap + res_sq)
        lowest = 0.5 * (ritz + curvature) - root_term
        first_coef = curvature - lowest
        pair_norm = jnp.sqrt(first_coef * first_coef + res_sq)
        fresh = vector[...] / length
        basis[...] = (first_coef * basis[...] - length * fresh) / pair_norm
        applied[...] = (first_coef * applied[...] - length * fresh_applied) / pair_norm
        ritz = lowest
    out_ref[...] = basis[...] * jnp.sqrt(jnp.float32(total_entries))
    energy_ref[...] = jnp.broadcast_to(ritz, energy_ref.shape)


def local(
    n_row, n_col, theta, left_env, right_env, left_sector, right_sector, term_on, left_size, right_size
):
    blocks, size, thin = theta.shape
    sectors, terms = left_env.shape[:2]
    row_index = lax.axis_index("row")
    col_index = lax.axis_index("col")
    own_left = lax.dynamic_slice_in_dim(left_sector, row_index * blocks, blocks)
    rows_live = lookup(left_size, own_left)
    cols_live = lookup(right_size, right_sector)
    col_ids = col_index * thin + jnp.arange(thin, dtype=jnp.int32)
    row_ids = jnp.arange(size, dtype=jnp.int32)
    mask = (
        (col_ids[None, :, None] < cols_live[:, None, None])
        & (row_ids[None, None, :] < rows_live[:, None, None])
    ).astype(jnp.float32)
    start = jnp.swapaxes(theta, 1, 2) * mask
    packed = pack_symmetric(left_env)
    half = size // 2
    steps = n_col // 2
    n_far = n_row // CORES - 1
    f32, bf16 = jnp.float32, jnp.bfloat16
    vmem = pl.BlockSpec(memory_space=pltpu.VMEM)
    smem = pl.BlockSpec(memory_space=pltpu.SMEM)
    anywhere = pl.BlockSpec(memory_space=pl.ANY)
    rights = right_env.shape[0]
    dma = pltpu.SemaphoreType.DMA
    new_theta, energy = pl.pallas_call(
        functools.partial(kernel, n_row, n_col, n_row * blocks * size * size),
        out_shape=(
            jax.ShapeDtypeStruct((blocks, thin, size), f32),
            jax.ShapeDtypeStruct((8, 128), f32),
        ),
        in_specs=[smem, smem, smem, vmem, vmem, anywhere, anywhere],
        out_specs=(vmem, vmem),
        scratch_shapes=[
            pltpu.VMEM((n_row * sectors, terms) + packed.shape[2:], f32),
            pltpu.VMEM((blocks * terms, size, size), bf16),
            pltpu.VMEM((blocks * terms, size, size), bf16),
            pltpu.VMEM((2, terms, size, size), f32),
            pltpu.VMEM((rights, terms, size, size), bf16),
            pltpu.VMEM((rights, terms, size, size), bf16),
            pltpu.VMEM((APPLIES, n_col, blocks, thin, size), f32),
            pltpu.VMEM((n_col, blocks, thin, size), f32),
            pltpu.VMEM((APPLIES, steps, blocks, thin, size), f32),
            pltpu.VMEM((APPLIES, steps, blocks, thin, size), f32),
            pltpu.VMEM((blocks, thin, size), f32),
            pltpu.VMEM((blocks, thin, size), f32),
            pltpu.VMEM((blocks, thin, size), f32),
            pltpu.VMEM((ROUNDS, n_row, 2, 8, 128), f32),
            pltpu.VMEM((ROUNDS, n_col, 2, 8, 128), f32),
            dma((2,)),
            dma,
            dma((n_far, sectors, 2)),
            dma((2,)),
            dma((n_far, sectors, 2)),
            dma((APPLIES, steps, 2, 2)),
            dma((APPLIES, steps, 2, 2)),
            dma((ROUNDS, n_row - 1, 2)),
            dma((ROUNDS, n_col - 1, 2)),
        ],
        compiler_params=pltpu.CompilerParams(
            collective_id=0, has_side_effects=True, vmem_limit_bytes=60 * 2**20
        ),
    )(own_left, right_sector, term_on.astype(f32), start, mask, packed, right_env)
    return jnp.swapaxes(new_theta, 1, 2), energy[0, 0]


def solution(mesh):
    placed = (
        P("row", None, "col"),
        P("row", "col", None, None),
        P(None, "col", None, None),
        P(),
        P("row"),
        P("row", "col"),
        P(),
        P(),
    )
    return jax.shard_map(
        functools.partial(local, mesh.shape["row"], mesh.shape["col"]),
        mesh=mesh,
        in_specs=placed,
        out_specs=(P("row", None, "col"), P()),
        check_vma=False,
    )
```

time: 835 us -> 254 us (0.30)
  waiting for transfers between devices: 474 us -> 0 us
  Pallas kernels: 0 us -> 241 us
  blocking collectives: 200 us -> 0 us
  matrix products: 72.3 us -> 0 us
  local copies, waits for them, and re-layouts: 29 us -> 3.77 us
  between operations: 25.2 us -> 0.68 us
  other arithmetic: 26.1 us -> 8.79 us
    pallas_call x0 -> x1, Pallas kernels: none -> 241 us  [local(): pl.pallas_call(functools.partial(kernel, n_row, n_col, n_row * blocks * s...]
    reduce_scatter x3 -> x0, waiting for transfers between devices: 201 us -> none  [operate(): lax.psum_scatter(contract(full_vector), 'col', scatter_dimension=2, tiled...]
    psum x5 -> x0, blocking collectives: 200 us -> none  [combine(): reduced = lax.psum(values, ('row', 'col'))]
    all_to_all x1 -> x0, waiting for transfers between devices: 174 us -> none  [local(): lax.all_to_all(outgoing, 'row', split_axis=0, concat_axis=0, tiled=True)]
    all_gather x3 -> x0, waiting for transfers between devices: 98.6 us -> none  [operate(): full_vector = lax.all_gather(vector, 'col', axis=2, tiled=True)]
    dot_general x6 -> x0, matrix products: 72.3 us -> none  [the longest x3 36.8 us: contract(): return jnp.einsum('swib,swjb->sij', middle, right_pick, precision=highest)]
    gather x3 -> x0, local copies, waits for them, and re-layouts: 27.6 us -> none  [the longest x1 10.1 us: local(): left_pick = jnp.take(arrived, position, axis=0)]
    mul x3 -> x1, other arithmetic: 13.3 us -> 1.75 us  [local(): start = jnp.swapaxes(theta, 1, 2) * mask]
  transfers between devices with their start and end apart: 7 -> 0, of which waited for: 6 -> 0; matrix products, arithmetic and copies ran while one was open for 2% -> 0% of each run, Pallas kernels for 0% -> 0%
where the time goes in v1:
time: 254 us
  Pallas kernels  241 us (95%)
  other arithmetic  8.79 us (3%)
  local copies, waits for them, and re-layouts  3.77 us (1%)
    pallas_call x1, Pallas kernels, local(): pl.pallas_call(functools.partial(kernel, n_row, n_col, n_row * blocks * s...  241 us

profile of v1, /device:TPU:0, one launch (start us, length us, event | category | flops | bytes accessed | tf_op | source)
XLA Modules:
  0.0 254.1 jit_solution(10175953011942261552)
XLA Ops:
  0.6 0.7 dynamic_slice.3.left_ref
  1.4 0.0 copy-start.1
  1.4 0.8 select_reduce_fusion.1
  2.2 0.1 iota_compare_fusion.2
  2.3 0.9 select_reduce_fusion.2
  3.1 0.1 broadcast_compare_fusion
  3.2 0.8 and_convert_fusion.mask_ref
  4.0 1.8 and_select_fusion.start_ref
  5.8 2.2 fusion
  8.0 0.0 copy-done.1
  8.0 0.0 copy-start
  8.0 0.1 pad.3.clone
  8.1 1.6 maximum_maximum_fusion.pack_ref
  9.7 0.0 copy-done
  9.7 0.1 copy.11
  9.8 0.6 convert_element_type.6.weight_ref
  10.4 240.9 %shard_map.95 = (f32[8,32,256]{2,1,0:T(8,128)}, f32[8,128]{1,0:T(8,128)}) custom-call(s32[8]{0:T(128)} %copy-done.1, s32[8]{0:T(128)} %right_ref.1, f32[8,4]{1,0:T(8,128)} %convert_element_type.6.weight_ref, f32[8,32,256]{2,1,0:T(8,128)} %and_select_fusion.start_ref, f32[8,32,256]{2,1,0:T(8,128)} %and_convert_fusion.mask_ref, ...), custom_call_target="tpu_custom_call" | custom-call | tf_op jit(solution)/shard_map/pallas_call | solution.py:400
  251.2 1.2 slice.15
  252.4 1.7 copy.13
  (3 shorter events, 0.0 us)
Async XLA Ops:
  1.4 6.6 %copy-start.1 = (s32[8]{0:T(128)}, s32[8]{0:T(128)S(1)}, u32[]{:S(2)}) copy-start(s32[8]{0:T(128)S(1)} %dynamic_slice.3.left_ref) | copy-start | bytes 100
  8.0 1.7 copy-start

commit v2 on v1

v2 whole, which is shorter than its diff:
```python
import functools

import jax
import jax.numpy as jnp
from jax import lax
from jax.experimental import pallas as pl
from jax.experimental.pallas import tpu as pltpu
from jax.sharding import PartitionSpec as P

ITERS = 2
APPLIES = ITERS + 1
ROUNDS = 2 * ITERS + 1
CORES = 2
GROUPS = 2
MESH = pl.DeviceIdType.MESH


def lookup(small_table, index_list):
    slot_hits = index_list[:, None] == jnp.arange(small_table.shape[0], dtype=jnp.int32)[None, :]
    return jnp.sum(jnp.where(slot_hits, small_table[None, :], 0), axis=1)


def pack_symmetric(tiles):
    half = tiles.shape[-1] // 2
    upper = tiles[..., :half, half:]
    first = tiles[..., :half, :half]
    second = tiles[..., half:, half:]
    rows = lax.broadcasted_iota(jnp.int32, (half, half), 0)
    cols = lax.broadcasted_iota(jnp.int32, (half, half), 1)
    both = jnp.where(rows <= cols, first, second)
    diag = jnp.sum(jnp.where(rows == cols, second, 0.0), axis=-2, keepdims=True)
    fill = jnp.zeros(tiles.shape[:-2] + (7, half), tiles.dtype)
    return jnp.concatenate([upper, both, diag, fill], axis=-2)


def split(x):
    high = x.astype(jnp.bfloat16)
    low = (x - high.astype(jnp.float32)).astype(jnp.bfloat16)
    return high, low


def tile_sum(x):
    cols = x.shape[-1]
    total = jnp.sum(x.reshape(-1, 8, cols), axis=0)
    return sum(total[:, i : i + 128] for i in range(0, cols, 128))


def kernel(
    n_row,
    n_col,
    total_entries,
    left_ref,
    right_ref,
    weight_ref,
    start_ref,
    mask_ref,
    pack_ref,
    env_ref,
    out_ref,
    energy_ref,
    gathered,
    left_parts,
    stage,
    right_parts,
    full,
    partial,
    from_right,
    from_left,
    basis,
    applied,
    vector,
    curve,
    row_sums,
    col_sums,
    env_sem,
    own_sem,
    far_sem,
    near_sem,
    pass_sem,
    gather_sem,
    scatter_sem,
    row_sem,
    col_sem,
):
    blocks, thin, size = start_ref.shape
    terms, sectors = pack_ref.shape[:2]
    half = size // 2
    group_blocks = blocks // GROUPS
    half_blocks = group_blocks // 2
    steps = n_col // 2
    n_far = n_row // CORES - 1
    me_row = lax.axis_index("row")
    me_col = lax.axis_index("col")

    def col_at(place):
        place = lax.rem(place + 2 * n_col, n_col)
        back = place // (n_col // 2)
        return (1 - back) * (2 * place) + back * (2 * n_col - 1 - 2 * place)

    odd = lax.rem(me_col, 2)
    place = (1 - odd) * (me_col // 2) + odd * (n_col - 1 - me_col // 2)
    right = col_at(place + 1)
    left = col_at(place - 1)

    def remote(src, dst, sems, row, col):
        return pltpu.make_async_remote_copy(
            src_ref=src,
            dst_ref=dst,
            send_sem=sems.at[0],
            recv_sem=sems.at[1],
            device_id=(row, col),
            device_id_type=MESH,
        )

    barrier = pltpu.get_barrier_semaphore()
    for step in range(1, n_row):
        peer = lax.rem(me_row + step, n_row)
        pl.semaphore_signal(barrier, inc=1, device_id=(peer, me_col), device_id_type=MESH)
    for step in range(1, n_col):
        peer = lax.rem(me_col + step, n_col)
        pl.semaphore_signal(barrier, inc=1, device_id=(me_row, peer), device_id_type=MESH)
    pl.semaphore_wait(barrier, n_row + n_col - 2)

    core = lax.rem(me_row, CORES)
    partner = me_row + 1 - 2 * core

    def sector_slots(term, row):
        return gathered[term].at[pl.ds(row * sectors, sectors)]

    far, near, own = [], [], []
    for term in range(terms):
        for step in range(1, n_far + 1):
            copy = remote(
                pack_ref.at[term],
                sector_slots(term, me_row),
                far_sem.at[term, step - 1],
                lax.rem(me_row + CORES * step, n_row),
                me_col,
            )
            copy.start()
            far.append(copy)
    for term in range(terms):
        here = sector_slots(term, me_row)
        near.append(remote(pack_ref.at[term], here, near_sem.at[term], partner, me_col))
        own.append(pltpu.make_async_copy(pack_ref.at[term], here, own_sem.at[term]))
        near[term].start()
        own[term].start()

    def gather(turn, group):
        first = group * group_blocks
        span = pl.ds(first, group_blocks)
        full[turn, me_col, span] = vector[span]
        sent, pair = [], ()
        for step in range(steps):
            for copy in pair:
                copy.wait_recv()
            last = step == steps - 1
            part_one = pl.ds(first, half_blocks) if last else span
            part_two = pl.ds(first + half_blocks, half_blocks) if last else span
            one = full.at[turn, col_at(place - step), part_one]
            two = full.at[turn, col_at(place + step), part_two]
            sems = gather_sem.at[turn, group, step]
            pair = (
                remote(one, one, sems.at[0], me_row, right),
                remote(two, two, sems.at[1], me_row, left),
            )
            for copy in pair:
                copy.start()
            sent.extend(pair)
            yield
        for copy in pair:
            copy.wait_recv()
        for copy in sent:
            copy.wait_send()

    def contract(turn, first, count, term_from, term_to, mode, length=None):
        def block_step(index, carry):
            block = first + index
            vec = full[turn, :, block].reshape(size, size)
            v_high, v_low = split(vec)
            left_side = jnp.concatenate([v_high, v_high, v_low], axis=1)
            middle = jnp.dot(
                left_side,
                left_parts[block, :, term_from * size : term_to * size],
                preferred_element_type=jnp.float32,
            )
            stack = []
            for term in range(term_from, term_to):
                at = (term - term_from) * size
                high, low = split(middle[:, at : at + size] * weight_ref[block, term])
                stack += [high, low, high]
            total = jnp.dot(
                right_parts[right_ref[block], :, 3 * term_from * size : 3 * term_to * size],
                jnp.concatenate(stack, axis=0),
                preferred_element_type=jnp.float32,
            )
            if mode == "product":
                curve[...] += tile_sum(((vec / length) * (total / length))[None])
            else:
                total = total.reshape(n_col, thin, size)
                if mode == "add":
                    total = total + partial[:, block]
                partial[:, block] = total
            return carry

        lax.fori_loop(0, count, block_step, 0)

    def scatter(turn, group):
        first = group * group_blocks
        span = pl.ds(first, group_blocks)
        part_one = pl.ds(first, half_blocks)
        part_two = pl.ds(first + half_blocks, half_blocks)
        sent, pair = [], ()
        for step in range(steps):
            for copy in pair:
                copy.wait_recv()
            low = col_at(place - steps + step)
            high = col_at(place + steps - step)
            if step > 0:
                one = part_one if step == 1 else span
                two = part_two if step == 1 else span
                partial[low, one] += from_right[turn, step - 1, one]
                partial[high, two] += from_left[turn, step - 1, two]
            one = part_one if step == 0 else span
            two = part_two if step == 0 else span
            sems = scatter_sem.at[turn, group, step]
            pair = (
                remote(
                    partial.at[low, one], from_right.at[turn, step, one], sems.at[0], me_row, left
                ),
                remote(
                    partial.at[high, two], from_left.at[turn, step, two], sems.at[1], me_row, right
                ),
            )
            for copy in pair:
                copy.start()
            sent.extend(pair)
            yield
        for copy in pair:
            copy.wait_recv()
        for copy in sent:
            copy.wait_send()

    def drain(*flows):
        flows = list(flows)
        while flows:
            for flow in list(flows):
                if next(flow, "end") == "end":
                    flows.remove(flow)

    def scattered(turn):
        last = steps - 1
        result = partial[me_col] + from_right[turn, last] + from_left[turn, last]
        return result * mask_ref[...]

    def combine(index, values):
        count = len(values)
        for i, value in enumerate(values):
            row_sums[index, me_row, i] = value
        copies = []
        for step in range(1, n_row):
            mine = row_sums.at[index, me_row, pl.ds(0, count)]
            peer = lax.rem(me_row + step, n_row)
            copies.append(remote(mine, mine, row_sem.at[index, step - 1], peer, me_col))
        for copy in copies:
            copy.start()
        for copy in copies:
            copy.wait_recv()
        for i in range(count):
            col_sums[index, me_col, i] = sum(row_sums[index, r, i] for r in range(n_row))
        more = []
        for step in range(1, n_col):
            mine = col_sums.at[index, me_col, pl.ds(0, count)]
            peer = lax.rem(me_col + step, n_col)
            more.append(remote(mine, mine, col_sem.at[index, step - 1], me_row, peer))
        for copy in more:
            copy.start()
        for copy in more:
            copy.wait_recv()
        for copy in copies + more:
            copy.wait_send()
        totals = [sum(col_sums[index, c, i] for c in range(n_col)) for i in range(count)]
        return [jnp.sum(total, axis=(0, 1), keepdims=True) for total in totals]

    def load_right():
        count = env_ref.shape[0]
        copies = [
            pltpu.make_async_copy(env_ref.at[i], stage.at[i % 2], env_sem.at[i % 2])
            for i in range(count)
        ]
        copies[0].start()
        for i in range(count):
            if i + 1 < count:
                copies[i + 1].start()
            copies[i].wait()
            for term in range(terms):
                high, low = split(stage[i % 2, term])
                for part, value in enumerate((high, high, low)):
                    at = (3 * term + part) * size
                    right_parts[i, :, at : at + size] = value

    forward = []

    def pass_left(term):
        for step in range(1, n_far + 1):
            source = lax.rem(me_row - CORES * step + n_row, n_row)
            far[term * n_far + step - 1].wait_recv()
            slots = sector_slots(term, source)
            copy = remote(slots, slots, pass_sem.at[term, step - 1], partner, me_col)
            copy.start()
            forward.append(copy)

    def load_left(term):
        own[term].wait()
        near[term].wait_recv()
        for copy in forward[term * n_far : (term + 1) * n_far]:
            copy.wait_recv()
        rows = lax.broadcasted_iota(jnp.int32, (half, half), 0)
        cols = lax.broadcasted_iota(jnp.int32, (half, half), 1)

        def unpack(block, carry):
            tile = gathered[term][left_ref[block]]
            upper = tile[:half]
            both = tile[half:size]
            flipped = both.T
            first = jnp.where(rows <= cols, both, flipped)
            second = jnp.where(rows > cols, both, flipped)
            second = jnp.where(rows == cols, tile[size : size + 1], second)
            quarters = (
                (0, 0, first),
                (0, half, upper),
                (half, 0, upper.T),
                (half, half, second),
            )
            for at_row, at_col, quarter in quarters:
                at = term * size + at_col
                high, low = split(quarter)
                for part, value in enumerate((high, low, high)):
                    top = part * size + at_row
                    left_parts[block, top : top + half, at : at + half] = value
            return carry

        lax.fori_loop(0, blocks, unpack, 0)

    vector[...] = start_ref[...]
    flows = [gather(0, group) for group in range(GROUPS)]
    for flow in flows:
        next(flow)
    load_right()
    drain(*flows)
    mid_term = terms // 2
    for term in range(mid_term):
        pass_left(term)
        load_left(term)
    for term in range(mid_term, terms):
        if term == mid_term:
            contract(0, 0, blocks, 0, mid_term, "set")
        pass_left(term)
        load_left(term)
    one, two = scatter(0, 0), scatter(0, 1)
    contract(0, 0, group_blocks, mid_term, terms, "add")
    next(one)
    contract(0, group_blocks, half_blocks, mid_term, terms, "add")
    next(one)
    contract(0, group_blocks + half_blocks, half_blocks, mid_term, terms, "add")
    drain(one, two)
    for copy in far + near + forward:
        copy.wait_send()
    image = scattered(0)
    start = start_ref[...]
    norm_sq, correlation = combine(0, (tile_sum(start * start), tile_sum(start * image)))
    inv_norm = 1.0 / jnp.sqrt(norm_sq)
    basis[...] = start * inv_norm
    applied[...] = image * inv_norm
    ritz = correlation / norm_sq
    for turn in range(1, ITERS + 1):
        vector[...] = applied[...] - ritz * basis[...]
        final = turn == ITERS
        mode = "product" if final else "set"
        one, two = gather(turn, 0), gather(turn, 1)
        next(one)
        (res_sq,) = combine(2 * turn - 1, (tile_sum(vector[...] * vector[...]),))
        length = jnp.sqrt(res_sq)
        for _ in range(steps - 1):
            next(one)
        next(two)
        drain(one)
        if final:
            curve[...] = jnp.zeros_like(curve)
        contract(turn, 0, half_blocks, 0, terms, mode, length)
        next(two)
        contract(turn, half_blocks, half_blocks, 0, terms, mode, length)
        next(two)
        if not final:
            back_one, back_two = scatter(turn, 0), scatter(turn, 1)
            next(back_one)
        drain(two)
        contract(turn, group_blocks, half_blocks, 0, terms, mode, length)
        if not final:
            next(back_one)
        contract(turn, group_blocks + half_blocks, half_blocks, 0, terms, mode, length)
        fresh = vector[...] / length
        if final:
            (curvature,) = combine(2 * turn, (curve[...],))
        else:
            drain(back_one, back_two)
            fresh_applied = scattered(turn) / length
            (curvature,) = combine(2 * turn, (tile_sum(fresh * fresh_applied),))
        half_gap = 0.5 * (ritz - curvature)
        root_term = jnp.sqrt(half_gap * half_gap + res_sq)
        lowest = 0.5 * (ritz + curvature) - root_term
        first_coef = curvature - lowest
        pair_norm = jnp.sqrt(first_coef * first_coef + res_sq)
        basis[...] = (first_coef * basis[...] - length * fresh) / pair_norm
        if not final:
            applied[...] = (first_coef * applied[...] - length * fresh_applied) / pair_norm
        ritz = lowest
    out_ref[...] = basis[...] * jnp.sqrt(jnp.float32(total_entries))
    energy_ref[...] = jnp.broadcast_to(ritz, energy_ref.shape)


def local(
    n_row, n_col, theta, left_env, right_env, left_sector, right_sector, term_on, left_size, right_size
):
    blocks, size, thin = theta.shape
    sectors, terms = left_env.shape[:2]
    row_index = lax.axis_index("row")
    col_index = lax.axis_index("col")
    own_left = lax.dynamic_slice_in_dim(left_sector, row_index * blocks, blocks)
    rows_live = lookup(left_size, own_left)
    cols_live = lookup(right_size, right_sector)
    col_ids = col_index * thin + jnp.arange(thin, dtype=jnp.int32)
    row_ids = jnp.arange(size, dtype=jnp.int32)
    mask = (
        (col_ids[None, :, None] < cols_live[:, None, None])
        & (row_ids[None, None, :] < rows_live[:, None, None])
    ).astype(jnp.float32)
    start = jnp.swapaxes(theta, 1, 2) * mask
    packed = jnp.swapaxes(pack_symmetric(left_env), 0, 1)
    steps = n_col // 2
    n_far = n_row // CORES - 1
    f32, bf16 = jnp.float32, jnp.bfloat16
    vmem = pl.BlockSpec(memory_space=pltpu.VMEM)
    smem = pl.BlockSpec(memory_space=pltpu.SMEM)
    anywhere = pl.BlockSpec(memory_space=pl.ANY)
    rights = right_env.shape[0]
    dma = pltpu.SemaphoreType.DMA
    new_theta, energy = pl.pallas_call(
        functools.partial(kernel, n_row, n_col, n_row * blocks * size * size),
        out_shape=(
            jax.ShapeDtypeStruct((blocks, thin, size), f32),
            jax.ShapeDtypeStruct((8, 128), f32),
        ),
        in_specs=[smem, smem, smem, vmem, vmem, anywhere, anywhere],
        out_specs=(vmem, vmem),
        scratch_shapes=[
            [pltpu.VMEM((n_row * sectors,) + packed.shape[2:], f32) for _ in range(terms)],
            pltpu.VMEM((blocks, 3 * size, terms * size), bf16),
            pltpu.VMEM((2, terms, size, size), f32),
            pltpu.VMEM((rights, size, 3 * terms * size), bf16),
            pltpu.VMEM((APPLIES, n_col, blocks, thin, size), f32),
            pltpu.VMEM((n_col, blocks, thin, size), f32),
            pltpu.VMEM((ITERS, steps, blocks, thin, size), f32),
            pltpu.VMEM((ITERS, steps, blocks, thin, size), f32),
            pltpu.VMEM((blocks, thin, size), f32),
            pltpu.VMEM((blocks, thin, size), f32),
            pltpu.VMEM((blocks, thin, size), f32),
            pltpu.VMEM((8, 128), f32),
            pltpu.VMEM((ROUNDS, n_row, 2, 8, 128), f32),
            pltpu.VMEM((ROUNDS, n_col, 2, 8, 128), f32),
            dma((2,)),
            dma((terms,)),
            dma((terms, n_far, 2)),
            dma((terms, 2)),
            dma((terms, n_far, 2)),
            dma((APPLIES, GROUPS, steps, 2, 2)),
            dma((ITERS, GROUPS, steps, 2, 2)),
            dma((ROUNDS, n_row - 1, 2)),
            dma((ROUNDS, n_col - 1, 2)),
        ],
        compiler_params=pltpu.CompilerParams(
            collective_id=0, has_side_effects=True, vmem_limit_bytes=60 * 2**20
        ),
    )(own_left, right_sector, term_on.astype(f32), start, mask, packed, right_env)
    return jnp.swapaxes(new_theta, 1, 2), energy[0, 0]


def solution(mesh):
    placed = (
        P("row", None, "col"),
        P("row", "col", None, None),
        P(None, "col", None, None),
        P(),
        P("row"),
        P("row", "col"),
        P(),
        P(),
    )
    return jax.shard_map(
        functools.partial(local, mesh.shape["row"], mesh.shape["col"]),
        mesh=mesh,
        in_specs=placed,
        out_specs=(P("row", None, "col"), P()),
        check_vma=False,
    )
```

time: 254 us -> 226 us (0.89)
  Pallas kernels: 241 us -> 215 us
  other arithmetic: 8.79 us -> 4.51 us
    pallas_call x1, Pallas kernels: 241 us -> 215 us  [local(): pl.pallas_call(functools.partial(kernel, n_row, n_col, n_row * blocks * s...]
where the time goes in v2:
time: 226 us; the launch traced here: 225 us
  Pallas kernels  215 us (95%)
  local copies, waits for them, and re-layouts  5.26 us (2%)
  other arithmetic  4.51 us (2%)
    pallas_call x1, Pallas kernels, local(): pl.pallas_call(functools.partial(kernel, n_row, n_col, n_row * blocks * s...  215 us

profile of v2, /device:TPU:0, one launch (start us, length us, event | category | flops | bytes accessed | tf_op | source)
XLA Modules:
  0.0 225.4 jit_solution(3451190731722771215)
XLA Ops:
  0.6 2.1 fusion
  2.8 0.2 copy_select_fusion
  3.0 0.0 copy-start.4
  3.0 0.0 copy-start.5
  3.0 0.0 copy-start.2
  3.0 0.0 copy-start.6
  3.0 0.1 pad.3.clone
  3.1 1.6 maximum_bitcast_fusion.pack_ref
  4.7 0.0 copy-done.4
  4.7 0.1 dynamic_slice.3.left_ref
  4.8 0.0 copy-done.5
  4.8 0.2 select_reduce_fusion.1
  5.0 0.1 iota_compare_fusion.2
  5.0 0.0 copy-done.2
  5.0 0.2 select_reduce_fusion.2
  5.2 0.1 broadcast_compare_fusion
  5.3 0.8 and_convert_fusion.mask_ref
  6.1 0.8 and_select_fusion.start_ref
  6.9 0.0 copy-done.1
  6.9 0.1 copy.14
  7.0 0.6 convert_element_type.6.weight_ref
  7.6 215.0 %shard_map.95 = (f32[8,32,256]{2,1,0:T(8,128)}, f32[8,128]{1,0:T(8,128)}) custom-call(s32[8]{0:T(128)} %copy-done.3, s32[8]{0:T(128)} %right_ref.1, f32[8,4]{1,0:T(8,128)} %convert_element_type.6.weight_ref, f32[8,32,256]{2,1,0:T(8,128)} %and_select_fusion.start_ref, f32[8,32,256]{2,1,0:T(8,128)} %and_convert_fusion.mask_ref, ...), custom_call_target="tpu_custom_call" | custom-call | tf_op jit(solution)/shard_map/pallas_call | solution.py:448
  222.6 1.2 slice.15
  223.8 1.7 copy.27
  (9 shorter events, 0.0 us)
Async XLA Ops:
  3.0 1.7 copy-start.4
  3.0 1.8 copy-start.5
  3.0 2.1 copy-start.2
  3.0 2.0 copy-start.6
  3.1 3.0 %copy-start = (f32[8,256,32]{1,2,0:T(8,128)S(1)}, f32[8,256,32]{1,2,0:T(8,128)}, u32[]{:S(2)}) copy-start(f32[8,256,32]{1,2,0:T(8,128)} %param.8) | copy-start | bytes 786436
  3.1 3.8 %copy-start.1 = (s32[8,4]{0,1:T(4,128)S(1)}, s32[8,4]{0,1:T(4,128)}, u32[]{:S(2)}) copy-start(s32[8,4]{0,1:T(4,128)} %param.13) | copy-start | bytes 388
  4.8 2.8 %copy-start.3 = (s32[8]{0:T(128)}, s32[8]{0:T(128)S(1)}, u32[]{:S(2)}) copy-start(s32[8]{0:T(128)S(1)} %dynamic_slice.3.left_ref) | copy-start | bytes 100

commit v3 on v2

--- a/solution.py
+++ b/solution.py
@@ -9,7 +9,7 @@
 
 ITERS = 2
 APPLIES = ITERS + 1
-ROUNDS = 2 * ITERS + 1
+ROUNDS = 2 * ITERS
 CORES = 2
 GROUPS = 2
 MESH = pl.DeviceIdType.MESH
@@ -66,9 +66,7 @@
     partial,
     from_right,
     from_left,
-    basis,
-    applied,
-    vector,
+    images,
     curve,
     row_sums,
     col_sums,
@@ -149,7 +147,7 @@
     def gather(turn, group):
         first = group * group_blocks
         span = pl.ds(first, group_blocks)
-        full[turn, me_col, span] = vector[span]
+        full[turn, me_col, span] = images[turn - 1, span] if turn else start_ref[span]
         sent, pair = [], ()
         for step in range(steps):
             for copy in pair:
@@ -173,10 +171,10 @@
         for copy in sent:
             copy.wait_send()
 
-    def contract(turn, first, count, term_from, term_to, mode, length=None):
+    def contract(turn, first, count, term_from, term_to, mode, formula, length=None):
         def block_step(index, carry):
             block = first + index
-            vec = full[turn, :, block].reshape(size, size)
+            vec = formula(*(full[i, :, block].reshape(size, size) for i in range(turn + 1)))
             v_high, v_low = split(vec)
             left_side = jnp.concatenate([v_high, v_high, v_low], axis=1)
             middle = jnp.dot(
@@ -248,12 +246,26 @@
                 if next(flow, "end") == "end":
                     flows.remove(flow)
 
-    def scattered(turn):
+    def chain(turn, group):
+        yield from scatter(turn, group)
         last = steps - 1
-        result = partial[me_col] + from_right[turn, last] + from_left[turn, last]
-        return result * mask_ref[...]
-
-    def combine(index, values):
+        span = pl.ds(group * group_blocks, group_blocks)
+        image = partial[me_col, span] + from_right[turn, last, span] + from_left[turn, last, span]
+        images[turn, span] = image * mask_ref[span]
+        yield from gather(turn + 1, group)
+
+    def ship(turn, rest):
+        one, two = chain(turn, 0), chain(turn, 1)
+        next(one)
+        rest(0)
+        next(one)
+        rest(1)
+        for _ in range(steps + 1):
+            next(one)
+            next(two)
+        return one, two
+
+    def combine(index, totals, values):
         count = len(values)
         for i, value in enumerate(values):
             row_sums[index, me_row, i] = value
@@ -264,6 +276,7 @@
             copies.append(remote(mine, mine, row_sem.at[index, step - 1], peer, me_col))
         for copy in copies:
             copy.start()
+        yield
         for copy in copies:
             copy.wait_recv()
         for i in range(count):
@@ -275,12 +288,14 @@
             more.append(remote(mine, mine, col_sem.at[index, step - 1], me_row, peer))
         for copy in more:
             copy.start()
+        yield
         for copy in more:
             copy.wait_recv()
         for copy in copies + more:
             copy.wait_send()
-        totals = [sum(col_sums[index, c, i] for c in range(n_col)) for i in range(count)]
-        return [jnp.sum(total, axis=(0, 1), keepdims=True) for total in totals]
+        for i in range(count):
+            total = sum(col_sums[index, c, i] for c in range(n_col))
+            totals.append(jnp.sum(total, axis=(0, 1), keepdims=True))
 
     def load_right():
         count = env_ref.shape[0]
@@ -342,7 +357,9 @@
 
         lax.fori_loop(0, blocks, unpack, 0)
 
-    vector[...] = start_ref[...]
+    def plain(start):
+        return start
+
     flows = [gather(0, group) for group in range(GROUPS)]
     for flow in flows:
         next(flow)
@@ -354,69 +371,97 @@
         load_left(term)
     for term in range(mid_term, terms):
         if term == mid_term:
-            contract(0, 0, blocks, 0, mid_term, "set")
+            contract(0, 0, blocks, 0, mid_term, "set", plain)
         pass_left(term)
         load_left(term)
-    one, two = scatter(0, 0), scatter(0, 1)
-    contract(0, 0, group_blocks, mid_term, terms, "add")
+    contract(0, 0, group_blocks, mid_term, terms, "add", plain)
+
+    def second_group(turn, *how):
+        def rest(part):
+            contract(turn, group_blocks + part * half_blocks, half_blocks, *how)
+
+        return rest
+
+    one, two = ship(0, second_group(0, mid_term, terms, "add", plain))
+    start, image = start_ref[...], images[0]
+    totals = []
+    sums = combine(0, totals, (tile_sum(start * start), tile_sum(start * image)))
+    next(sums)
     next(one)
-    contract(0, group_blocks, half_blocks, mid_term, terms, "add")
-    next(one)
-    contract(0, group_blocks + half_blocks, half_blocks, mid_term, terms, "add")
-    drain(one, two)
+    next(two)
+    next(sums)
+    drain(one)
+    next(two)
+    drain(sums)
     for copy in far + near + forward:
         copy.wait_send()
-    image = scattered(0)
-    start = start_ref[...]
-    norm_sq, correlation = combine(0, (tile_sum(start * start), tile_sum(start * image)))
+    norm_sq, correlation = totals
     inv_norm = 1.0 / jnp.sqrt(norm_sq)
-    basis[...] = start * inv_norm
-    applied[...] = image * inv_norm
     ritz = correlation / norm_sq
-    for turn in range(1, ITERS + 1):
-        vector[...] = applied[...] - ritz * basis[...]
-        final = turn == ITERS
-        mode = "product" if final else "set"
-        one, two = gather(turn, 0), gather(turn, 1)
-        next(one)
-        (res_sq,) = combine(2 * turn - 1, (tile_sum(vector[...] * vector[...]),))
-        length = jnp.sqrt(res_sq)
-        for _ in range(steps - 1):
-            next(one)
-        next(two)
-        drain(one)
-        if final:
-            curve[...] = jnp.zeros_like(curve)
-        contract(turn, 0, half_blocks, 0, terms, mode, length)
-        next(two)
-        contract(turn, half_blocks, half_blocks, 0, terms, mode, length)
-        next(two)
-        if not final:
-            back_one, back_two = scatter(turn, 0), scatter(turn, 1)
-            next(back_one)
-        drain(two)
-        contract(turn, group_blocks, half_blocks, 0, terms, mode, length)
-        if not final:
-            next(back_one)
-        contract(turn, group_blocks + half_blocks, half_blocks, 0, terms, mode, length)
-        fresh = vector[...] / length
-        if final:
-            (curvature,) = combine(2 * turn, (curve[...],))
-        else:
-            drain(back_one, back_two)
-            fresh_applied = scattered(turn) / length
-            (curvature,) = combine(2 * turn, (tile_sum(fresh * fresh_applied),))
+
+    def first_residual(start, image):
+        return image * inv_norm - ritz * (start * inv_norm)
+
+    residual = first_residual(start_ref[...], images[0])
+    totals = []
+    sums = combine(1, totals, (tile_sum(residual * residual),))
+    next(sums)
+    contract(1, 0, half_blocks, 0, terms, "set", first_residual)
+    next(two)
+    next(sums)
+    contract(1, half_blocks, half_blocks, 0, terms, "set", first_residual)
+    drain(two, sums)
+    (res_sq,) = totals
+    length = jnp.sqrt(res_sq)
+
+    one, two = ship(1, second_group(1, 0, terms, "set", first_residual))
+    fresh = first_residual(start_ref[...], images[0]) / length
+    totals = []
+    sums = combine(2, totals, (tile_sum(fresh * (images[1] / length)),))
+    next(sums)
+    next(one)
+    next(two)
+    next(sums)
+    drain(one)
+    next(two)
+    drain(sums)
+    (curvature,) = totals
+
+    def rotation(ritz, curvature, res_sq):
         half_gap = 0.5 * (ritz - curvature)
         root_term = jnp.sqrt(half_gap * half_gap + res_sq)
         lowest = 0.5 * (ritz + curvature) - root_term
         first_coef = curvature - lowest
         pair_norm = jnp.sqrt(first_coef * first_coef + res_sq)
-        basis[...] = (first_coef * basis[...] - length * fresh) / pair_norm
-        if not final:
-            applied[...] = (first_coef * applied[...] - length * fresh_applied) / pair_norm
-        ritz = lowest
-    out_ref[...] = basis[...] * jnp.sqrt(jnp.float32(total_entries))
-    energy_ref[...] = jnp.broadcast_to(ritz, energy_ref.shape)
+        return lowest, first_coef, 1.0 / pair_norm
+
+    lowest, first_coef, inv_pair = rotation(ritz, curvature, res_sq)
+
+    def second_basis(start, image):
+        return (first_coef * (start * inv_norm) - first_residual(start, image)) * inv_pair
+
+    def second_residual(start, image, next_image):
+        applied = (first_coef * (image * inv_norm) - next_image) * inv_pair
+        return applied - lowest * second_basis(start, image)
+
+    curve[...] = jnp.zeros_like(curve)
+    how = (0, terms, "product", second_residual, length)
+    contract(2, 0, half_blocks, *how)
+    next(two)
+    contract(2, half_blocks, half_blocks, *how)
+    drain(two)
+    contract(2, group_blocks, group_blocks, *how)
+    residual = second_residual(start_ref[...], images[0], images[1])
+    totals = []
+    drain(combine(3, totals, (tile_sum(residual * residual), curve[...])))
+    next_res_sq, product = totals
+    scale = length / jnp.sqrt(next_res_sq)
+    energy, next_coef, next_inv = rotation(lowest, product * scale * scale, next_res_sq)
+    basis = second_basis(start_ref[...], images[0])
+    residual = second_residual(start_ref[...], images[0], images[1])
+    basis = (next_coef * basis - residual) * next_inv
+    out_ref[...] = basis * jnp.sqrt(jnp.float32(total_entries))
+    energy_ref[...] = jnp.broadcast_to(energy, energy_ref.shape)
 
 
 def local(
@@ -462,9 +507,7 @@
             pltpu.VMEM((n_col, blocks, thin, size), f32),
             pltpu.VMEM((ITERS, steps, blocks, thin, size), f32),
             pltpu.VMEM((ITERS, steps, blocks, thin, size), f32),
-            pltpu.VMEM((blocks, thin, size), f32),
-            pltpu.VMEM((blocks, thin, size), f32),
-            pltpu.VMEM((blocks, thin, size), f32),
+            pltpu.VMEM((ITERS, blocks, thin, size), f32),
             pltpu.VMEM((8, 128), f32),
             pltpu.VMEM((ROUNDS, n_row, 2, 8, 128), f32),
             pltpu.VMEM((ROUNDS, n_col, 2, 8, 128), f32),

time: 226 us -> 190 us (0.84)
  Pallas kernels: 215 us -> 179 us
    pallas_call x1, Pallas kernels: 215 us -> 179 us  [local(): pl.pallas_call(functools.partial(kernel, n_row, n_col, n_row * blocks * s...]
where the time goes in v3:
time: 190 us; the launch traced here: 189 us
  Pallas kernels  179 us (94%)
  local copies, waits for them, and re-layouts  5.26 us (3%)
  other arithmetic  4.51 us (2%)
    pallas_call x1, Pallas kernels, local(): pl.pallas_call(functools.partial(kernel, n_row, n_col, n_row * blocks * s...  179 us

profile of v3, /device:TPU:0, one launch (start us, length us, event | category | flops | bytes accessed | tf_op | source)
XLA Modules:
  0.0 189.5 jit_solution(7990516272009647525)
XLA Ops:
  0.6 2.1 %fusion = (f32[4,4,128,128]{3,2,1,0:T(8,128)S(1)}, f32[4,4,128,128]{3,2,1,0:T(8,128)S(1)}, f32[4,4,128,128]{3,2,1,0:T(8,128)S(1)}) fusion(f32[4,4,256,256]{3,2,1,0:T(8,128)} %param.9), kind=kLoop, calls=%fused_computation.14 | loop fusion | bytes 6291456 | tf_op jit(solution)/shard_map/slice | solution.py:25
  2.8 0.2 copy_select_fusion
  3.0 0.0 copy-start.4
  3.0 0.0 copy-start.5
  3.0 0.0 copy-start.2
  3.0 0.0 copy-start.6
  3.0 0.1 pad.3.clone
  3.1 1.6 maximum_bitcast_fusion.pack_ref
  4.7 0.0 copy-done.4
  4.7 0.1 dynamic_slice.3.left_ref
  4.8 0.0 copy-done.5
  4.8 0.2 select_reduce_fusion.1
  5.0 0.1 iota_compare_fusion.2
  5.0 0.0 copy-done.2
  5.0 0.2 select_reduce_fusion.2
  5.2 0.1 broadcast_compare_fusion
  5.3 0.8 and_convert_fusion.mask_ref
  6.1 0.8 and_select_fusion.start_ref
  6.9 0.0 copy-done.1
  6.9 0.1 copy.14
  7.0 0.6 convert_element_type.6.weight_ref
  7.6 179.0 %shard_map.95 = (f32[8,32,256]{2,1,0:T(8,128)}, f32[8,128]{1,0:T(8,128)}) custom-call(s32[8]{0:T(128)} %copy-done.3, s32[8]{0:T(128)} %right_ref.1, f32[8,4]{1,0:T(8,128)} %convert_element_type.6.weight_ref, f32[8,32,256]{2,1,0:T(8,128)} %and_select_fusion.start_ref, f32[8,32,256]{2,1,0:T(8,128)} %and_convert_fusion.mask_ref, ...), custom_call_target="tpu_custom_call" | custom-call | tf_op jit(solution)/shard_map/pallas_call | solution.py:493
  186.6 1.2 slice.15
  187.8 1.7 copy.27
  (9 shorter events, 0.0 us)
Async XLA Ops:
  3.0 1.7 copy-start.4
  3.0 1.8 copy-start.5
  3.0 2.1 %copy-start.2 = (s32[8]{0:T(128)S(1)}, s32[8]{0:T(128)}, u32[]{:S(2)}) copy-start(s32[8]{0:T(128)} %right_ref.1) | copy-start | bytes 100
  3.0 2.0 %copy-start.6 = (s32[8]{0:T(128)S(1)}, s32[8]{0:T(128)}, u32[]{:S(2)}) copy-start(s32[8]{0:T(128)} %param.15) | copy-start | bytes 100
  3.1 3.0 %copy-start = (f32[8,256,32]{1,2,0:T(8,128)S(1)}, f32[8,256,32]{1,2,0:T(8,128)}, u32[]{:S(2)}) copy-start(f32[8,256,32]{1,2,0:T(8,128)} %param.8) | copy-start | bytes 786436
  3.1 3.8 %copy-start.1 = (s32[8,4]{0,1:T(4,128)S(1)}, s32[8,4]{0,1:T(4,128)}, u32[]{:S(2)}) copy-start(s32[8,4]{0,1:T(4,128)} %param.13) | copy-start | bytes 388
  4.8 2.8 %copy-start.3 = (s32[8]{0:T(128)}, s32[8]{0:T(128)S(1)}, u32[]{:S(2)}) copy-start(s32[8]{0:T(128)S(1)} %dynamic_slice.3.left_ref) | copy-start | bytes 100

commit v4 on v3

--- a/solution.py
+++ b/solution.py
@@ -185,7 +185,7 @@
             stack = []
             for term in range(term_from, term_to):
                 at = (term - term_from) * size
-                high, low = split(middle[:, at : at + size] * weight_ref[block, term])
+                high, low = split(middle[:, at : at + size] * weight_ref[block, term].astype(jnp.float32))
                 stack += [high, low, high]
             total = jnp.dot(
                 right_parts[right_ref[block], :, 3 * term_from * size : 3 * term_to * size],
@@ -365,7 +365,7 @@
         next(flow)
     load_right()
     drain(*flows)
-    mid_term = terms // 2
+    mid_term = terms - 1
     for term in range(mid_term):
         pass_left(term)
         load_left(term)
@@ -461,7 +461,7 @@
     residual = second_residual(start_ref[...], images[0], images[1])
     basis = (next_coef * basis - residual) * next_inv
     out_ref[...] = basis * jnp.sqrt(jnp.float32(total_entries))
-    energy_ref[...] = jnp.broadcast_to(energy, energy_ref.shape)
+    energy_ref[...] = energy
 
 
 def local(
@@ -494,7 +494,7 @@
         functools.partial(kernel, n_row, n_col, n_row * blocks * size * size),
         out_shape=(
             jax.ShapeDtypeStruct((blocks, thin, size), f32),
-            jax.ShapeDtypeStruct((8, 128), f32),
+            jax.ShapeDtypeStruct((1, 1), f32),
         ),
         in_specs=[smem, smem, smem, vmem, vmem, anywhere, anywhere],
         out_specs=(vmem, vmem),
@@ -524,8 +524,8 @@
         compiler_params=pltpu.CompilerParams(
             collective_id=0, has_side_effects=True, vmem_limit_bytes=60 * 2**20
         ),
-    )(own_left, right_sector, term_on.astype(f32), start, mask, packed, right_env)
-    return jnp.swapaxes(new_theta, 1, 2), energy[0, 0]
+    )(own_left, right_sector, term_on, start, mask, packed, right_env)
+    return jnp.swapaxes(new_theta, 1, 2), energy.reshape(())
 
 
 def solution(mesh):

time: 190 us -> 190 us (level)
  no operation moved by 1% of the time
where the time goes in v4:
time: 190 us
  Pallas kernels  179 us (94%)
  local copies, waits for them, and re-layouts  4.66 us (2%)
  other arithmetic  3.91 us (2%)
  between operations  2.51 us (1%)
    pallas_call x1, Pallas kernels, local(): pl.pallas_call(functools.partial(kernel, n_row, n_col, n_row * blocks * s...  179 us

profile of v4, /device:TPU:0, one launch (start us, length us, event | category | flops | bytes accessed | tf_op | source)
XLA Modules:
  0.0 189.9 jit_solution(12171158285350958423)
XLA Ops:
  0.6 2.1 %fusion = (f32[4,4,128,128]{3,2,1,0:T(8,128)S(1)}, f32[4,4,128,128]{3,2,1,0:T(8,128)S(1)}, f32[4,4,128,128]{3,2,1,0:T(8,128)S(1)}) fusion(f32[4,4,256,256]{3,2,1,0:T(8,128)} %param.9), kind=kLoop, calls=%fused_computation.14 | loop fusion | bytes 6291456 | tf_op jit(solution)/shard_map/slice | solution.py:25
  2.8 0.2 copy_select_fusion
  3.0 0.0 copy-start.4
  3.0 0.0 copy-start.5
  3.0 0.0 copy-start.2
  3.0 0.0 copy-start.6
  3.0 0.1 pad.3.clone
  3.1 1.6 maximum_bitcast_fusion.pack_ref
  4.7 0.0 copy-done.4
  4.7 0.1 dynamic_slice.3.left_ref
  4.8 0.0 copy-done.5
  4.8 0.2 select_reduce_fusion.1
  5.0 0.1 iota_compare_fusion.2
  5.0 0.0 copy-done.2
  5.0 0.0 copy-done.6
  5.0 0.2 select_reduce_fusion.2
  5.2 0.1 broadcast_compare_fusion
  5.3 0.8 and_convert_fusion.mask_ref
  6.1 0.0 copy-done
  6.1 0.8 and_select_fusion.start_ref
  6.9 0.0 copy-done.1
  6.9 0.7 copy.17.weight_ref
  7.6 178.9 %shard_map.95 = (f32[8,32,256]{2,1,0:T(8,128)}, f32[1,1]{1,0:T(1,128)}) custom-call(s32[8]{0:T(128)} %copy-done.3, s32[8]{0:T(128)} %right_ref.1, s32[8,4]{1,0:T(8,128)} %copy.17.weight_ref, f32[8,32,256]{2,1,0:T(8,128)} %and_select_fusion.start_ref, f32[8,32,256]{2,1,0:T(8,128)} %and_convert_fusion.mask_ref, ...), custom_call_target="tpu_custom_call" | custom-call | tf_op jit(solution)/shard_map/pallas_call | solution.py:493
  186.5 1.7 copy.28
  (7 shorter events, 0.0 us)
Async XLA Ops:
  3.0 1.7 copy-start.4
  3.0 1.8 copy-start.5
  3.0 2.1 %copy-start.2 = (s32[8]{0:T(128)S(1)}, s32[8]{0:T(128)}, u32[]{:S(2)}) copy-start(s32[8]{0:T(128)} %right_ref.1) | copy-start | bytes 100
  3.0 2.0 %copy-start.6 = (s32[8]{0:T(128)S(1)}, s32[8]{0:T(128)}, u32[]{:S(2)}) copy-start(s32[8]{0:T(128)} %param.15) | copy-start | bytes 100
  3.1 3.0 %copy-start = (f32[8,256,32]{1,2,0:T(8,128)S(1)}, f32[8,256,32]{1,2,0:T(8,128)}, u32[]{:S(2)}) copy-start(f32[8,256,32]{1,2,0:T(8,128)} %param.8) | copy-start | bytes 786436
  3.1 3.8 %copy-start.1 = (s32[8,4]{0,1:T(4,128)S(1)}, s32[8,4]{0,1:T(4,128)}, u32[]{:S(2)}) copy-start(s32[8,4]{0,1:T(4,128)} %param.13) | copy-start | bytes 388
  4.8 2.8 %copy-start.3 = (s32[8]{0:T(128)}, s32[8]{0:T(128)S(1)}, u32[]{:S(2)}) copy-start(s32[8]{0:T(128)S(1)} %dynamic_slice.3.left_ref) | copy-start | bytes 100
